TPU v7x, 128 devices: a whole 4x4x4 slice. The times are simulated.
128 devices in a mesh: dp: 32 (over y, x_hi, z), tensor: 4 (over x_lo, core).
Axes of the slice: x: 4 (x_hi: 2, x_lo: 2; x = x_hi * 2 + x_lo), y: 4, z: 4, core: 2. Of those that a mesh axis runs over, the one named last changes fastest.
Arguments:
- prompt_x: bfloat16 [4096, 5120], P('dp', 'tensor'), may hold values from -6 to 6
- prompt_bc: bfloat16 [4096, 512], P('dp'), may hold values from -6 to 6
- prompt_dt: float32 [80, 4096], P('tensor', 'dp'), may hold values from -2.5 to 6.5
- prompt_z: bfloat16 [4096, 5120], P('dp', 'tensor'), may hold values from -6 to 6
- resp_x: bfloat16 [16384, 5120], P('dp', 'tensor'), may hold values from -6 to 6
- resp_bc: bfloat16 [16384, 512], P('dp'), may hold values from -6 to 6
- resp_dt: float32 [80, 16384], P('tensor', 'dp'), may hold values from -2.5 to 6.5
- resp_z: bfloat16 [16384, 5120], P('dp', 'tensor'), may hold values from -6 to 6
- conv_x: float32 [4, 5120], P(None, 'tensor'), may hold values from -3 to 3
- conv_bc: float32 [4, 512], replicated, may hold values from -3 to 3
- head_params: float32 [3, 80], P(None, 'tensor'), may hold values from -8 to 1.5, as said below
- prompt_of: int32 [32], replicated, may hold values from 0 to 31, each once
- resp_len: int32 [32, 4], P('dp'), may hold values from 32 to 128, as said below
- prompt_cot: bfloat16 [4096, 5120], P('dp', 'tensor'), may hold values from -6 to 6
- resp_cot: bfloat16 [16384, 5120], P('dp', 'tensor'), may hold values from -6 to 6
Outputs:
- resp_out: bfloat16 [16384, 5120], P('dp', 'tensor')
- prompt_grad_x: bfloat16 [4096, 5120], P('dp', 'tensor')
- prompt_grad_bc: float32 [4096, 512], P('dp')
- prompt_grad_dt: float32 [80, 4096], P('tensor', 'dp')
- resp_grad_x: bfloat16 [16384, 5120], P('dp', 'tensor')
- resp_grad_bc: float32 [16384, 512], P('dp')
- resp_grad_dt: float32 [80, 16384], P('tensor', 'dp')
- conv_x_grad: float32 [4, 5120], P(None, 'tensor')
- conv_bc_grad: float32 [4, 512], replicated
- head_grads: float32 [3, 80], P(None, 'tensor')
Inputs may be any that keep to these rules, and one draw needn't show every extreme that they name: prompt_of is a permutation: every prompt is continued on exactly one dp index. `resp_len`: every dp index has at least one response of the full 128 tokens. `head_params`: row 0 is a log rate, row 1 a step bias below zero, row 2 a skip gain.
All inputs are finite; a program needn't handle non-finite values.
Results may differ from a plain program's by a relative error of at most 0.0045.
Values sent between devices are 32-bit elements; how exact they have to be, the bound alone decides.
A program may use at most 192 MiB of HBM per device.

v0:
```python
import math

import jax
import jax.numpy as jnp
from jax import lax
from jax.sharding import PartitionSpec as P

HEAD = 64
CONV = 4
SPAN = 128


def conv_silu(raw_rows, trailing_rows, kernel):
    extended = jnp.concatenate([trailing_rows, raw_rows], axis=0)
    length = raw_rows.shape[0]
    summed = jnp.zeros(raw_rows.shape, jnp.float32)
    for offset in range(kernel.shape[0]):
        summed = summed + kernel[offset][None, :] * extended[offset : offset + length]
    return jax.nn.silu(summed)


def state_mixer(feat_conv, proj_conv, step_raw, gate_rows, params, start_state):
    head_count = params.shape[1]
    state_dim = proj_conv.shape[1] // 2
    length = feat_conv.shape[0]
    blocks = length // SPAN
    step_size = jax.nn.softplus(step_raw + params[1][:, None])
    log_decay = -jnp.exp(params[0])[:, None] * step_size
    feat_blocks = feat_conv.reshape(blocks, SPAN, head_count, HEAD)
    write_blocks = proj_conv[:, :state_dim].reshape(blocks, SPAN, state_dim)
    read_blocks = proj_conv[:, state_dim:].reshape(blocks, SPAN, state_dim)
    step_blocks = step_size.reshape(head_count, blocks, SPAN).transpose(1, 0, 2)
    rate_blocks = log_decay.reshape(head_count, blocks, SPAN).transpose(1, 0, 2)
    lower = jnp.arange(SPAN)[:, None] >= jnp.arange(SPAN)[None, :]
    skip_gain = params[2][None, :, None]

    def advance(carry_state, block):
        feat_rows, write_rows, read_rows, step_rows, rate_rows = block
        cumulative = jnp.cumsum(rate_rows, axis=1)
        differ = cumulative[:, :, None] - cumulative[:, None, :]
        within = jnp.where(lower[None], jnp.exp(jnp.minimum(differ, 0.0)), 0.0)
        scores = jnp.dot(read_rows, write_rows.T, precision=lax.Precision.HIGHEST)
        mixing = scores[None] * within * step_rows[:, None, :]
        inside = jnp.einsum("hts,shp->thp", mixing, feat_rows, precision=lax.Precision.HIGHEST)
        carried = jnp.einsum("tn,hpn->thp", read_rows, carry_state, precision=lax.Precision.HIGHEST)
        carried = carried * jnp.exp(cumulative).T[:, :, None]
        outputs = inside + carried + skip_gain * feat_rows
        leaving = (jnp.exp(cumulative[:, -1:] - cumulative) * step_rows).T
        update = jnp.einsum(
            "sn,shp->hpn",
            write_rows,
            feat_rows * leaving[:, :, None],
            precision=lax.Precision.HIGHEST,
        )
        carry_state = jnp.exp(cumulative[:, -1])[:, None, None] * carry_state + update
        return (carry_state, outputs)

    final_state, outputs = lax.scan(
        jax.checkpoint(advance),
        start_state,
        (feat_blocks, write_blocks, read_blocks, step_blocks, rate_blocks),
    )
    mixed = outputs.reshape(length, head_count * HEAD) * jax.nn.silu(gate_rows)
    return (mixed, final_state)


def pack_flat(pieces):
    joined = jnp.concatenate([piece.reshape(-1) for piece in pieces])
    members = lax.axis_size("dp") * lax.axis_size("tensor")
    padding = -joined.shape[0] % members
    return joined


def unpack_flat(joined, layouts):
    pieces = []
    offset = 0
    for layout in layouts:
        amount = math.prod(layout)
        pieces.append(joined[offset : offset + amount].reshape(layout))
        offset = offset + amount
    return pieces


def relay_states(joined, source_of):
    members = lax.axis_size("dp")
    holding = lax.all_to_all(
        joined.reshape(members, -1), "dp", split_axis=0, concat_axis=0, tiled=True
    )
    chosen = jnp.take(holding, source_of, axis=0)
    return lax.all_to_all(chosen, "dp", split_axis=0, concat_axis=0, tiled=True).reshape(-1)


def body(
    prompt_x,
    prompt_bc,
    prompt_dt,
    prompt_z,
    resp_x,
    resp_bc,
    resp_dt,
    resp_z,
    conv_x,
    conv_bc,
    head_params,
    prompt_of,
    resp_len,
    prompt_cot,
    resp_cot,
):
    channels = prompt_x.shape[1]
    bc_width = prompt_bc.shape[1]
    head_count = head_params.shape[1]
    responses = resp_len.shape[1]
    length = resp_x.shape[0] // responses
    prompt_rows = prompt_x.shape[0]
    tail_len = CONV - 1
    prompt_feat = prompt_x.astype(jnp.float32)
    prompt_proj = prompt_bc.astype(jnp.float32)
    prompt_gate = prompt_z.astype(jnp.float32)
    zero_feat = jnp.zeros((tail_len, channels), jnp.float32)
    zero_proj = jnp.zeros((tail_len, bc_width), jnp.float32)
    zero_state = jnp.zeros((head_count, HEAD, bc_width // 2), jnp.float32)
    layouts = ((head_count, HEAD, bc_width // 2), (tail_len, channels), (tail_len, bc_width))
    prompt_fconv, pull_pfeat = jax.vjp(
        lambda raw_rows, kernel: conv_silu(raw_rows, zero_feat, kernel), prompt_feat, conv_x
    )
    prompt_pconv, pull_pproj = jax.vjp(
        lambda raw_rows, kernel: conv_silu(raw_rows, zero_proj, kernel), prompt_proj, conv_bc
    )
    prompt_pair, pull_pmix = jax.vjp(
        lambda feat_conv, proj_conv, step_raw, params: state_mixer(
            feat_conv, proj_conv, step_raw, prompt_gate, params, zero_state
        ),
        prompt_fconv,
        prompt_pconv,
        prompt_dt,
        head_params,
    )
    outgoing = pack_flat((prompt_pair[1], prompt_feat[-tail_len:], prompt_proj[-tail_len:]))
    start_state, tail_feat, tail_proj = unpack_flat(relay_states(outgoing, prompt_of), layouts)
    resp_feat = resp_x.astype(jnp.float32).reshape(responses, length, channels)
    resp_proj = resp_bc.astype(jnp.float32).reshape(responses, length, bc_width)
    resp_gate = resp_z.astype(jnp.float32).reshape(responses, length, channels)
    resp_steps = resp_dt.reshape(head_count, responses, length).transpose(1, 0, 2)

    def conv_all(raw_set, trailing_rows, kernel):
        return lax.map(lambda single: conv_silu(single, trailing_rows, kernel), raw_set)

    def mix_all(feat_set, proj_set, step_set, params, begin_state):
        return lax.map(
            lambda single: state_mixer(
                single[0], single[1], single[2], single[3], params, begin_state
            )[0],
            (feat_set, proj_set, step_set, resp_gate),
        )

    resp_fconv, pull_rfeat = jax.vjp(conv_all, resp_feat, tail_feat, conv_x)
    resp_pconv, pull_rproj = jax.vjp(conv_all, resp_proj, tail_proj, conv_bc)
    resp_mixed, pull_rmix = jax.vjp(
        mix_all, resp_fconv, resp_pconv, resp_steps, head_params, start_state
    )
    resp_out = resp_mixed.reshape(-1, channels).astype(jnp.bfloat16)
    live_mask = (jnp.arange(length)[None, :] < resp_len[0][:, None]).astype(jnp.float32)
    resp_cotan = (
        resp_cot.astype(jnp.float32).reshape(responses, length, channels) * live_mask[:, :, None]
    )
    d_rfconv, d_rpconv, d_rsteps, d_rparams, d_start = pull_rmix(resp_cotan)
    d_rfeat, d_tail_feat, d_conv_feat_r = pull_rfeat(d_rfconv)
    d_rpconv = lax.psum(d_rpconv, "tensor")
    response_projection_grad, d_tail_proj, d_conv_proj_r = pull_rproj(d_rpconv)
    members = prompt_of.shape[0]
    inverse = jnp.sum(
        jnp.arange(members)[:, None] * (prompt_of[:, None] == jnp.arange(members)[None, :]), axis=0
    )
    returning = pack_flat((d_start, d_tail_feat, d_tail_proj))
    d_final, d_last_feat, d_last_proj = unpack_flat(relay_states(returning, inverse), layouts)
    d_pfconv, d_ppconv, d_psteps, d_pparams = pull_pmix((prompt_cot.astype(jnp.float32), d_final))
    d_pfeat, d_conv_feat_p = pull_pfeat(d_pfconv)
    d_pfeat = d_pfeat + jnp.pad(d_last_feat, ((prompt_rows - tail_len, 0), (0, 0)))
    d_ppconv = lax.psum(d_ppconv, "tensor")
    d_pproj, d_conv_proj_p = pull_pproj(d_ppconv)
    d_pproj = d_pproj + jnp.pad(d_last_proj, ((prompt_rows - tail_len, 0), (0, 0)))
    conv_proj_part = d_conv_proj_r + d_conv_proj_p
    conv_x_grad, conv_bc_grad, head_grads = lax.psum(
        (d_conv_feat_r + d_conv_feat_p, conv_proj_part, d_rparams + d_pparams), "dp"
    )
    return (
        resp_out,
        d_pfeat.astype(jnp.bfloat16),
        d_pproj,
        d_psteps,
        d_rfeat.reshape(-1, channels).astype(jnp.bfloat16),
        response_projection_grad.reshape(-1, bc_width),
        d_rsteps.transpose(1, 0, 2).reshape(head_count, -1),
        conv_x_grad,
        conv_bc_grad,
        head_grads,
    )


def solution(mesh):
    placed = (
        P("dp", "tensor"),
        P("dp", None),
        P("tensor", "dp"),
        P("dp", "tensor"),
        P("dp", "tensor"),
        P("dp", None),
        P("tensor", "dp"),
        P("dp", "tensor"),
        P(None, "tensor"),
        P(),
        P(None, "tensor"),
        P(),
        P("dp", None),
        P("dp", "tensor"),
        P("dp", "tensor"),
    )
    return jax.shard_map(
        body,
        mesh=mesh,
        in_specs=placed,
        out_specs=(
            P("dp", "tensor"),
            P("dp", "tensor"),
            P("dp", None),
            P("tensor", "dp"),
            P("dp", "tensor"),
            P("dp", None),
            P("tensor", "dp"),
            P(None, "tensor"),
            P(),
            P(None, "tensor"),
        ),
        check_vma=False,
    )
```

profile of v0, /device:TPU:0, one launch (start us, length us, event | category | flops | bytes accessed | tf_op | source)
XLA Modules:
  0.0 738.0 jit_solution(7179357367075729459)
XLA Ops:
  22.8 11.0 %all-to-all-start = ((f32[32,1,10408]{2,1,0:T(1,128)}), f32[32,1,10408]{2,1,0:T(1,128)S(1)}, u32[]{:S(2)}, u32[]{:S(2)}) async-start(f32[32,1,10408]{2,1,0:T(1,128)} %all_to_all.28), calls=%async_computation | async-start | bytes 2686976 | tf_op jit(solution)/shard_map/all_to_all | solution.py:86
  33.8 20.9 %all-to-all-done = f32[32,1,10408]{2,1,0:T(1,128)S(1)} async-done(((f32[32,1,10408]{2,1,0:T(1,128)}), f32[32,1,10408]{2,1,0:T(1,128)S(1)}, u32[]{:S(2)}, u32[]{:S(2)}) %all-to-all-start) | async-done | bytes 1332256 | tf_op jit(solution)/shard_map/all_to_all | solution.py:86
  58.5 5.4 all-to-all-start.1
  74.0 9.7 %all-to-all-done.1 = f32[32,1,10408]{2,1,0:T(1,128)} async-done(((f32[32,1,10408]{2,1,0:T(1,128)}), f32[32,1,10408]{2,1,0:T(1,128)}, u32[]{:S(2)}, u32[]{:S(2)}) %all-to-all-start.1) | async-done | bytes 1332256 | tf_op jit(solution)/shard_map/all_to_all | solution.py:90
  83.7 5.6 reduce.14
  106.0 13.2 %while.180 = (s32[]{:T(128)}, f32[4,128,1280]{2,1,0:T(8,128)}, f32[4,128,1280]{2,1,0:T(8,128)}, f32[4,128,1280]{2,1,0:T(8,128)}, f32[4,128,1280]{2,1,0:T(8,128)}...) while((s32[]{:T(128)}, f32[4,128,1280]{2,1,0:T(8,128)}, ...), condition=%wide.region_2.4_spmd.clone, body=%wide.region_1.3_spmd.sunk.clone | while | flops 2949122 | bytes 8613017 | solution.py:147
  127.2 12.2 %while.181 = (s32[]{:T(128)}, f32[4,128,512]{2,1,0:T(8,128)}, f32[4,128,512]{2,1,0:T(8,128)}, f32[4,128,512]{2,1,0:T(8,128)}, f32[4,128,512]{2,1,0:T(8,128)}, /*...) while((s32[]{:T(128)}, f32[4,128,512]{2,1,0:T(8,128)}, ...), condition=%wide.region_4.6_spmd.clone, body=%wide.region_3.5_spmd.sunk.clone | while | flops 1179650 | bytes 3429513 | solution.py:147
  142.9 75.5 %while.182 = (s32[]{:T(128)}, bf16[4,128,1280]{1,2,0:T(8,128)(2,1)}, f32[4,20,128]{2,1,0:T(8,128)}, f32[4,20,128]{2,1,0:T(8,128)}, f32[4,1,20,64,256]{4,3,2,1,0:...) while((s32[]{:T(128)}, bf16[4,128,1280]{1,2,0:T(8,128)(2,1)}, ...), condition=%wide.region_7.9_spmd.clone.clone, body=%wide.region_5.8_spmd.clone.sunk.clone | while | flops 809635328 | bytes 18214504 | solution.py:150
  149.5 4.8 fusion.314
  168.3 4.8 fusion.314
  187.2 4.8 fusion.314
  206.1 4.8 fusion.314
  221.8 140.1 %while.183 = (s32[]{:T(128)}, f32[3,20]{1,0:T(4,128)}, f32[20,64,256]{2,1,0:T(8,128)}, f32[4,128,1280]{1,2,0:T(8,128)}, f32[4,128,512]{2,1,0:T(8,128)}, /*index=...) while((s32[]{:T(128)}, f32[3,20]{1,0:T(4,128)}, ...), condition=%wide.region_22.24_spmd.clone.clone, body=%wide.region_8.23_spmd.clone.sunk.clone | while | flops 3183853312 | bytes 42879304 | solution.py:150
  361.9 26.8 %while.184 = (s32[]{:T(128)}, f32[3,1280]{1,0:T(4,128)}, f32[4,1280]{1,0:T(4,128)}, bf16[4,128,1280]{2,1,0:T(8,128)(2,1)}, f32[1,1280]{1,0:T(1,128)}, /*index=5*...) while((s32[]{:T(128)}, f32[3,1280]{1,0:T(4,128)}, ...), condition=%wide.region_28.30_spmd.clone.clone, body=%wide.region_23.29_spmd.clone.sunk.clone | while | flops 3152644 | bytes 18278824 | solution.py:147
  391.6 8.4 %all-reduce.54.cloned.1.call-done = f32[4,128,512]{2,1,0:T(8,128)} async-done(((f32[4,128,512]{2,1,0:T(8,128)}), f32[4,128,512]{2,1,0:T(8,128)}) %all-reduce.54.cloned.1.call-update) | async-done | bytes 1048592 | tf_op jit(solution)/shard_map/psum | solution.py:169
  401.1 11.0 %while.185 = (s32[]{:T(128)}, f32[3,512]{1,0:T(4,128)S(1)}, f32[4,512]{1,0:T(4,128)S(1)}, f32[4,128,512]{2,1,0:T(8,128)}, f32[1,512]{1,0:T(1,128)S(1)}, /*index=...) while((s32[]{:T(128)}, f32[3,512]{1,0:T(4,128)S(1)}, ...), condition=%wide.region_35.37_spmd.clone.clone, body=%wide.region_30.36_spmd.clone.sunk.clone | while | flops 1261060 | bytes 6082740 | solution.py:147
  415.8 9.5 %all-to-all-start.2 = ((f32[32,1,10408]{2,1,0:T(1,128)}), f32[32,1,10408]{2,1,0:T(1,128)S(1)}, u32[]{:S(2)}, u32[]{:S(2)}) async-start(f32[32,1,10408]{2,1,0:T(1,128)} %all_to_all.33), calls=%async_computation.2 | async-start | bytes 2686976 | tf_op jit(solution)/shard_map/all_to_all | solution.py:86
  425.4 21.2 %all-to-all-done.2 = f32[32,1,10408]{2,1,0:T(1,128)S(1)} async-done(((f32[32,1,10408]{2,1,0:T(1,128)}), f32[32,1,10408]{2,1,0:T(1,128)S(1)}, u32[]{:S(2)}, u32[]{:S(2)}) %all-to-all-start.2) | async-done | bytes 1332256 | tf_op jit(solution)/shard_map/all_to_all | solution.py:86
  450.4 5.4 all-to-all-start.3
  460.6 15.1 %all-to-all-done.3 = f32[32,1,10408]{2,1,0:T(1,128)S(1)} async-done(((f32[32,1,10408]{2,1,0:T(1,128)}), f32[32,1,10408]{2,1,0:T(1,128)S(1)}, u32[]{:S(2)}, u32[]{:S(2)}) %all-to-all-start.3) | async-done | bytes 1332256 | tf_op jit(solution)/shard_map/all_to_all | solution.py:90
  475.7 4.6 reduce.15
  497.5 5.0 fusion.166
  521.4 23.5 %all-reduce.56.cloned.1.call-done = f32[128,512]{1,0:T(8,128)} async-done(((f32[128,512]{1,0:T(8,128)}), f32[128,512]{1,0:T(8,128)}) %all-reduce.56.cloned.1.call-update) | async-done | bytes 262160 | tf_op jit(solution)/shard_map/psum | solution.py:180
  546.4 183.4 %all-reduce.50 = (f32[4,1280]{1,0:T(4,128)}, f32[4,512]{1,0:T(4,128)}, f32[3,20]{1,0:T(4,128)}) all-reduce(f32[4,1280]{1,0:T(4,128)S(1)} %copy-done.81, f32[4,512]{1,0:T(4,128)S(1)} %add_add_fusion.3, f32[3,20]{1,0:T(4,128)S(1)} %add_add_fusion.4), channel_id=1, replica_groups=mesh['dp'=32,'tensor'=4] {'dp'}, use_global_device_ids=true, to_apply=%region_52.54 | all-reduce | flops 7228 | bytes 57824 | tf_op jit(solution)/shard_map/psum | solution.py:184
  (944 shorter events, 371.1 us)
Async XLA Ops:
  22.8 11.0 %copy-start.114 = (s32[32]{0:T(128)S(1)}, s32[32]{0:T(128)}, u32[]{:S(2)}) copy-start(s32[32]{0:T(128)} %param.40) | copy-start | bytes 388
  22.8 32.0 %all-to-all-start = ((f32[32,1,10408]{2,1,0:T(1,128)}), f32[32,1,10408]{2,1,0:T(1,128)S(1)}, u32[]{:S(2)}, u32[]{:S(2)}) async-start(f32[32,1,10408]{2,1,0:T(1,128)} %all_to_all.28), calls=%async_computation | async-start | bytes 2686976 | tf_op jit(solution)/shard_map/all_to_all | solution.py:86
  58.5 25.2 %all-to-all-start.1 = ((f32[32,1,10408]{2,1,0:T(1,128)}), f32[32,1,10408]{2,1,0:T(1,128)}, u32[]{:S(2)}, u32[]{:S(2)}) async-start(f32[32,1,10408]{2,1,0:T(1,128)} %copy.106), calls=%async_computation.1 | async-start | bytes 2686976 | tf_op jit(solution)/shard_map/all_to_all | solution.py:90
  63.9 336.1 %all-reduce.54.cloned.1.call-start = ((), (), s32[]{:S(2)}) async-start(), calls=%async_computation.4 | async-start | bytes 2097152 | tf_op jit(solution)/shard_map/psum | solution.py:169
  127.2 12.2 %slice-start.2 = ((f32[333056]{0:T(1024)}), f32[327680]{0:T(1024)S(1)}, s32[]{:S(2)}) async-start(f32[333056]{0:T(1024)} %reshape.718), calls=%async_computation.8 | async-start | bytes 2621440 | tf_op jit(solution)/shard_map/slice | solution.py:79
  236.7 12.1 %copy-start.68 = (f32[20]{0:T(128)}, f32[20]{0:T(128)S(1)}, u32[]{:S(2)}) copy-start(f32[20]{0:T(128)S(1)} %get-tuple-element.3443) | copy-start | bytes 244 | tf_op jit(solution)/shard_map/transpose(jvp())/while
  270.6 12.1 %copy-start.68 = (f32[20]{0:T(128)}, f32[20]{0:T(128)S(1)}, u32[]{:S(2)}) copy-start(f32[20]{0:T(128)S(1)} %get-tuple-element.3443) | copy-start | bytes 244 | tf_op jit(solution)/shard_map/transpose(jvp())/while
  305.8 12.1 %copy-start.68 = (f32[20]{0:T(128)}, f32[20]{0:T(128)S(1)}, u32[]{:S(2)}) copy-start(f32[20]{0:T(128)S(1)} %get-tuple-element.3443) | copy-start | bytes 244 | tf_op jit(solution)/shard_map/transpose(jvp())/while
  341.0 12.1 %copy-start.68 = (f32[20]{0:T(128)}, f32[20]{0:T(128)S(1)}, u32[]{:S(2)}) copy-start(f32[20]{0:T(128)S(1)} %get-tuple-element.3443) | copy-start | bytes 244 | tf_op jit(solution)/shard_map/transpose(jvp())/while
  389.5 11.7 %copy-start.48 = (f32[1,512]{1,0:T(1,128)S(1)}, f32[1,512]{1,0:T(1,128)}, u32[]{:S(2)}) copy-start(f32[1,512]{1,0:T(1,128)} %copy-done.47) | copy-start | bytes 6148
  389.5 11.7 %copy-start.51 = (f32[1,512]{1,0:T(1,128)S(1)}, f32[1,512]{1,0:T(1,128)}, u32[]{:S(2)}) copy-start(f32[1,512]{1,0:T(1,128)} %copy-done.50) | copy-start | bytes 6148
  389.5 11.6 %copy-start.54 = (f32[1,512]{1,0:T(1,128)S(1)}, f32[1,512]{1,0:T(1,128)}, u32[]{:S(2)}) copy-start(f32[1,512]{1,0:T(1,128)} %copy-done.53) | copy-start | bytes 6148
  389.5 11.6 %copy-start.61 = (f32[3,512]{1,0:T(4,128)S(1)}, f32[3,512]{1,0:T(4,128)}, u32[]{:S(2)}) copy-start(f32[3,512]{1,0:T(4,128)} %custom-call.4) | copy-start | bytes 18436
  389.5 11.6 %copy-start.62 = (f32[4,512]{1,0:T(4,128)S(1)}, f32[4,512]{1,0:T(4,128)}, u32[]{:S(2)}) copy-start(f32[4,512]{1,0:T(4,128)} %custom-call.5) | copy-start | bytes 24580
  415.8 30.9 %all-to-all-start.2 = ((f32[32,1,10408]{2,1,0:T(1,128)}), f32[32,1,10408]{2,1,0:T(1,128)S(1)}, u32[]{:S(2)}, u32[]{:S(2)}) async-start(f32[32,1,10408]{2,1,0:T(1,128)} %all_to_all.33), calls=%async_computation.2 | async-start | bytes 2686976 | tf_op jit(solution)/shard_map/all_to_all | solution.py:86
  450.4 25.3 %all-to-all-start.3 = ((f32[32,1,10408]{2,1,0:T(1,128)}), f32[32,1,10408]{2,1,0:T(1,128)S(1)}, u32[]{:S(2)}, u32[]{:S(2)}) async-start(f32[32,1,10408]{2,1,0:T(1,128)} %copy.116), calls=%async_computation.3 | async-start | bytes 2686976 | tf_op jit(solution)/shard_map/all_to_all | solution.py:90
  455.8 89.1 %all-reduce.56.cloned.1.call-start = ((), (), s32[]{:S(2)}) async-start(), calls=%async_computation.5 | async-start | bytes 524288 | tf_op jit(solution)/shard_map/psum | solution.py:180
  517.3 27.6 %copy-start.20 = (f32[128,512]{1,0:T(8,128)S(1)}, f32[128,512]{1,0:T(8,128)}, u32[]{:S(2)}) copy-start(f32[128,512]{1,0:T(8,128)} %copy-done.19) | copy-start | bytes 786436
  518.8 27.5 %copy-start.46 = (f32[1,512]{1,0:T(1,128)S(1)}, f32[1,512]{1,0:T(1,128)}, u32[]{:S(2)}) copy-start(f32[1,512]{1,0:T(1,128)} %copy-done.45) | copy-start | bytes 6148
  518.8 27.5 %copy-start.49 = (f32[1,512]{1,0:T(1,128)S(1)}, f32[1,512]{1,0:T(1,128)}, u32[]{:S(2)}) copy-start(f32[1,512]{1,0:T(1,128)} %copy-done.47) | copy-start | bytes 6148
  518.8 27.5 %copy-start.52 = (f32[1,512]{1,0:T(1,128)S(1)}, f32[1,512]{1,0:T(1,128)}, u32[]{:S(2)}) copy-start(f32[1,512]{1,0:T(1,128)} %copy-done.50) | copy-start | bytes 6148
  518.8 27.5 %copy-start.55 = (f32[1,512]{1,0:T(1,128)S(1)}, f32[1,512]{1,0:T(1,128)}, u32[]{:S(2)}) copy-start(f32[1,512]{1,0:T(1,128)} %copy-done.53) | copy-start | bytes 6148
  521.4 25.0 %copy-start.64 = (f32[4,512]{1,0:T(4,128)S(1)}, f32[4,512]{1,0:T(4,128)}, u32[]{:S(2)}) copy-start(f32[4,512]{1,0:T(4,128)} %copy-done.63) | copy-start | bytes 24580
  521.4 25.1 %copy-start.81 = (f32[4,1280]{1,0:T(4,128)S(1)}, f32[4,1280]{1,0:T(4,128)}, u32[]{:S(2)}) copy-start(f32[4,1280]{1,0:T(4,128)} %add_add_fusion.2) | copy-start | bytes 61444
  (218 other events, 534.7 us)
Sparse Core Ops, SparseCore 0:
  362.0 37.9 all-reduce.53
  512.0 32.7 all-reduce.55
where the time goes:
time: 749 us; the launch traced here: 738 us
  blocking collectives  183 us (24%)
  other arithmetic  154 us (21%)
  local copies, waits for them, and re-layouts  142 us (19%)
  matrix products  109 us (15%)
  waiting for transfers between devices  99 us (13%)
  starting transfers between devices  31.5 us (4%)
  between operations  15.7 us (2%)
    psum x1, blocking collectives, body(): lax.psum((d_conv_feat_r + d_conv_feat_p, conv_proj_part, d_rparams + d_pp...  183 us
    dot_general x14, matrix products, advance(): jnp.einsum('hts,shp->thp', mixing, feat_rows, precision=lax.Precision.HIG...  48.4 us
    dynamic_update_slice x36, other arithmetic, conv_all(): lax.map(lambda single: conv_silu(single, trailing_rows, kernel), raw_set)  42.9 us
    all_to_all x2, waiting for transfers between devices, relay_states(): lax.all_to_all(joined.reshape(members, -1), 'dp', split_axis=0, concat_ax...  42.2 us
    dot_general x18, matrix products, advance(): jnp.einsum('tn,hpn->thp', read_rows, carry_state, precision=lax.Precision...  34.1 us
    another operation x25, local copies, waits for them, and re-layouts  27.9 us
    all_to_all x2, waiting for transfers between devices, relay_states(): lax.all_to_all(chosen, 'dp', split_axis=0, concat_axis=0, tiled=True)  24.8 us
    psum x1, waiting for transfers between devices, body(): d_ppconv = lax.psum(d_ppconv, 'tensor')  23.5 us
  transfers between devices with their start and end apart: 6, of which 6 were waited for; matrix products, arithmetic and copies ran while one was open for 6% of the time, Pallas kernels for 0%

commit v1 on v0

v1 whole, which is shorter than its diff:
```python
import functools
import types

import jax
import jax.numpy as jnp
from jax import lax
from jax.experimental import pallas as pl
from jax.experimental.pallas import tpu as pltpu
from jax.sharding import PartitionSpec as P

F32 = jnp.float32
BF = jnp.bfloat16
T = 128
NH = 20
NG = 10
NS = 256
CHD = 1280
BCW = 512
CHUNK = 48


def mm(a, b, ca, cb):
    return lax.dot_general(a, b, (((ca,), (cb,)), ((), ())), preferred_element_type=F32)


def split2(a):
    hi = a.astype(BF)
    return hi, (a - hi.astype(F32)).astype(BF)


def split3(a):
    hi = a.astype(BF)
    rest = a - hi.astype(F32)
    mid = rest.astype(BF)
    return hi, mid, (rest - mid.astype(F32)).astype(BF)


def mm3(a, b, ca, cb):
    ah, al = split2(a)
    bh, bl = split2(b)
    return mm(ah, bh, ca, cb) + mm(ah, bl, ca, cb) + mm(al, bh, ca, cb)


def mmx(a, ones, ca, cb):
    hi, mid, lo = split3(a)
    return mm(hi, ones, ca, cb) + mm(mid, ones, ca, cb) + mm(lo, ones, ca, cb)


def sigmoid(v):
    return 0.5 + 0.5 * jnp.tanh(0.5 * v)


def softplus(u):
    e = jnp.exp(-jnp.abs(u))
    s = e / (2.0 + e)
    q = s * s
    poly = 1.0 + q * (1 / 3 + q * (1 / 5 + q * (1 / 7 + q * (1 / 9 + q * (1 / 11 + q / 13)))))
    return jnp.maximum(u, 0.0) + 2.0 * s * poly


def iota(shape, dim):
    return lax.broadcasted_iota(jnp.int32, shape, dim)


def fold8(a):
    return jnp.sum(a.reshape(16, 8, 128), axis=0)


IN = (
    "px", "pbc", "pdt", "pz", "pcot", "rx", "rbc", "rdt", "rz", "rcot", "cw", "cbc", "hp", "of", "inv", "rlen",
)
OUT = (
    "o_out", "o_pdx", "o_pdbc", "o_pddt", "o_rdx", "o_rdbc", "o_rddt", "o_cw", "o_cbc", "o_hp",
)


def scratch_table(n):
    v = pltpu.VMEM
    dma = pltpu.SemaphoreType.DMA
    return dict(
        fs=v((n, CHUNK, 128), F32), fh=v((n, CHUNK, 128), F32), fl=v((n, CHUNK, 128), F32), fr=v((n, CHUNK, 128), F32),
        bs=v((n, CHUNK, 128), F32), bh=v((n, CHUNK, 128), F32), bl=v((n, CHUNK, 128), F32), br=v((n, CHUNK, 128), F32),
        ts=v((32, 2, 128), F32), th=v((32, 2, 128), F32), tl=v((32, 2, 128), F32), tr=v((32, 2, 128), F32),
        us=v((32, 2, 128), F32), uh=v((32, 2, 128), F32), ul=v((32, 2, 128), F32), ur=v((32, 2, 128), F32),
        ps=v((32, 2, 128), F32), ph=v((32, 2, 128), F32), pr=v((32, 2, 128), F32),
        rsum=v((512, BCW), F32), rrecv=v((2, 256, BCW), F32),
        psum=v((144, BCW), F32), pfull=v((144, BCW), F32), precv=v((2, 72, BCW), F32),
        dtr=v((5, NH, T), F32), sig=v((5, NH, T), F32), lr=v((5, NH, T), F32), cumr=v((5, NH, T), F32),
        tmp=v((128, 128), F32), col=v((2, NH, 1), F32), dex=v((1, CHD), F32),
        cumB=v((5 * NH, T, T), F32), dtE=v((5 * T, CHD), F32),
        R=v((NG, 512, 128), BF),
        B=v((5, T, NS), F32), C=v((5, T, NS), F32), Cb=v((5, T, NS), BF), gpb=v((5 * T, BCW), F32),
        G=v((5, T, T), F32), dG=v((5, T, T), F32), acc=v((5, T, 128), F32), accq=v((T, 128), F32),
        xs=v((136, 128), F32), ds=v((144, 128), F32),
        tailx=v((8, CHD), F32), tailb=v((8, BCW), F32), dtailx=v((8, CHD), F32), dtailb=v((8, BCW), F32),
        dw=v((4, 8, CHD), F32), dwb=v((4, 8, BCW), F32), dD=v((8, CHD), F32),
        pxc=v((T, CHD), F32), pgp=v((T, CHD), F32), pdy=v((T, CHD), F32), pdxd=v((T, CHD), F32),
        yl=v((512, CHD), F32), edy=v((512, CHD), BF), ee=v((512, CHD), F32),
        S=v((CHD, NS), BF), dS=v((CHD, NS), BF),
        dlr=v((NH, T), F32), ddr=v((NH, T), F32),
        sem=dma((8, 2, 32)), tsem=dma((6, 2)),
    )


def kernel(n, nt, *refs):
    names = list(IN) + list(OUT) + list(scratch_table(n))
    K = types.SimpleNamespace(**dict(zip(names, refs)))
    me = lax.axis_index("dp")
    mt = lax.axis_index("tensor")
    left = iota((T, 128), 1) < 64

    def spread(src, dst, sem, width=None):
        def copy(k):
            peer = lax.rem(me + k, n)
            return pltpu.make_async_remote_copy(
                src_ref=src(peer), dst_ref=dst, send_sem=K.sem.at[sem, 0, k], recv_sem=K.sem.at[sem, 1, k],
                device_id={"dp": peer}, device_id_type=pl.DeviceIdType.MESH,
            )

        return copy

    def each_peer(action):
        if n > 1:
            pl.loop(1, n)(action)

    def start_all(copy):
        each_peer(lambda k: copy(k).start())

    def wait_all(copy):
        each_peer(lambda k: copy(k).wait())

    def choose(table, hold, sel):
        if n == 1:
            source = {id(K.th): K.ts, id(K.fh): K.fs, id(K.bh): K.bs, id(K.uh): K.us}[id(hold)]
            target = {id(K.th): K.tr, id(K.fh): K.fr, id(K.bh): K.br, id(K.uh): K.ur}[id(hold)]
            target[...] = source[...]
            sel[...] = source[...]
            return

        def one(d):
            sel[d] = hold[table[d]]

        pl.loop(0, n)(one)

    if n > 1:
        barrier = pltpu.get_barrier_semaphore()

        def greet(k):
            pl.semaphore_signal(
                barrier, inc=1, device_id={"dp": lax.rem(me + k, n)}, device_id_type=pl.DeviceIdType.MESH
            )

        each_peer(greet)
        for k in range(1, nt):
            pl.semaphore_signal(
                barrier, inc=1, device_id={"tensor": lax.rem(mt + k, nt)}, device_id_type=pl.DeviceIdType.MESH
            )

    tail_tile_x = K.px[112:128, :].astype(F32)
    tail_tile_b = K.pbc[112:128, :].astype(F32)
    K.ts[...] = jnp.zeros((32, 2, 128), F32)
    for r in range(42):
        i, m = divmod(r, 14)
        part = tail_tile_x[13 + i : 14 + i, 128 * m : 128 * m + 128] if m < 10 else (
            tail_tile_b[13 + i : 14 + i, 128 * (m - 10) : 128 * (m - 10) + 128]
        )
        K.ts[r // 2, r % 2 : r % 2 + 1, :] = part

    t1 = spread(lambda p: K.ts.at[p], K.th.at[me], 0)
    if n > 1:
        pl.semaphore_wait(barrier, n - 1 + nt - 1)
    start_all(t1)

    tri = (iota((T, T), 0) <= iota((T, T), 1)).astype(F32).astype(BF)
    trir = (iota((T, T), 0) >= iota((T, T), 1)).astype(F32).astype(BF)
    tris = (iota((T, T), 0) < iota((T, T), 1)).astype(F32).astype(BF)
    lower = iota((T, T), 0) >= iota((T, T), 1)
    eye = iota((NH, NH), 0) == iota((NH, NH), 1)

    def column(row):
        return jnp.sum(jnp.where(eye, jnp.broadcast_to(K.hp[row : row + 1, :], (NH, NH)), 0.0), axis=1, keepdims=True)

    K.col[0] = -jnp.exp(column(0))
    K.col[1] = column(1)
    left1 = iota((1, 128), 1) < 64
    for g in range(NG):
        K.dex[:, 128 * g : 128 * g + 128] = jnp.where(
            left1, K.hp[2:3, 2 * g : 2 * g + 1], K.hp[2:3, 2 * g + 1 : 2 * g + 2]
        )

    def make_R(g):
        r = iota((512, 128), 0)
        lane = iota((512, 128), 1)
        want = 2 * g + jnp.where((r & 127) >= 64, 1, 0) + jnp.where(r >= 256, 32, 0)
        K.R[g] = (lane == want).astype(F32).astype(BF)

    pl.loop(0, NG)(make_R)
    for name in ("dG", "acc", "accq", "dw", "dwb", "dD", "dtailx", "dtailb", "dlr", "ddr", "ds", "tmp"):
        ref = getattr(K, name)
        ref[...] = jnp.zeros(ref.shape, F32)

    def step_tables(dt_ref, at, q):
        u = dt_ref[:, pl.ds(pl.multiple_of(at * T, T), T)] + K.col[1]
        dt = softplus(u)
        lr = K.col[0] * dt
        cum = mmx(lr, tri, 1, 0)
        K.dtr[q] = dt
        K.sig[q] = 1.0 / (1.0 + jnp.exp(-u))
        K.lr[q] = lr
        K.cumr[q] = cum
        K.tmp[0:NH, :] = cum
        K.tmp[32 : 32 + NH, :] = dt
        cols = K.tmp[...].T
        for h in range(NH):
            K.cumB[q * NH + h] = jnp.broadcast_to(cols[:, h : h + 1], (T, T))
        for g in range(NG):
            a = 32 + 2 * g
            K.dtE[pl.ds(pl.multiple_of(q * T, T), T), 128 * g : 128 * g + 128] = jnp.where(
                left, jnp.broadcast_to(cols[:, a : a + 1], (T, 128)), jnp.broadcast_to(cols[:, a + 1 : a + 2], (T, 128))
            )

    def conv(x, tail, w):
        K.xs[0:8, :] = tail
        K.xs[8:136, :] = x
        v = w[0] * K.xs[5:133, :] + w[1] * K.xs[6:134, :] + w[2] * K.xs[7:135, :] + w[3] * x
        s = sigmoid(v)
        xc = v * s
        return xc, s + xc * (1.0 - s)

    def conv_back(dv, w, dw_ref, lanes, tail_ref):
        K.ds[8:136, :] = dv
        dx = w[3] * dv + w[2] * K.ds[9:137, :] + w[1] * K.ds[10:138, :] + w[0] * K.ds[11:139, :]
        for k in range(4):
            x = K.xs[5 + k : 133 + k, :]
            dw_ref[k, :, lanes] += fold8(dv * x)
        if tail_ref is not None:
            tail_ref[:, lanes] += w[0] * K.ds[3:11, :] + w[1] * K.ds[2:10, :] + w[2] * K.ds[1:9, :]
        return dx

    def taps(ref, lanes):
        return [ref[k : k + 1, lanes] for k in range(4)]

    def lanes_of(g):
        return pl.ds(pl.multiple_of(g * 128, 128), 128)

    def rows_of(q):
        return pl.ds(pl.multiple_of(q * T, T), T)

    def bc_forward(bc_ref, at, q, tail):
        for m in range(4):
            lanes = slice(128 * m, 128 * m + 128)
            xc, gp = conv(bc_ref[rows_of(at), lanes].astype(F32), tail(lanes), taps(K.cbc, lanes))
            K.gpb[rows_of(q), lanes] = gp
            if m < 2:
                K.B[q, :, lanes] = xc
            else:
                half = slice(128 * (m - 2), 128 * (m - 2) + 128)
                K.C[q, :, half] = xc
                K.Cb[q, :, half] = xc.astype(BF)
        K.G[q] = jnp.where(lower, mm3(K.C[q], K.B[q], 1, 1), 0.0)

    def cum_pair(q, g):
        return jnp.where(left, K.cumB[q * NH + 2 * g], K.cumB[q * NH + 2 * g + 1])

    def attend(q, g, xc, dy, dt):
        xd = dt * xc
        x2 = jnp.concatenate([jnp.where(left, xd, 0.0).astype(BF), jnp.where(left, 0.0, xd).astype(BF)], axis=0)
        d2 = jnp.concatenate([jnp.where(left, dy, 0.0).astype(BF), jnp.where(left, 0.0, dy).astype(BF)], axis=0)
        xdb = xd.astype(BF)
        dyb = dy.astype(BF)
        scores = K.G[q]
        decay = [
            jnp.exp(jnp.minimum(K.cumB[q * NH + 2 * g + i] - K.cumr[q, pl.ds(2 * g + i, 1), :], 0.0)) for i in range(2)
        ]
        mix = [(scores * one).astype(BF) for one in decay]
        yin = mm(jnp.concatenate(mix, axis=1), x2, 1, 0)
        dxd = mm(jnp.concatenate(mix, axis=0), d2, 0, 0)
        dmix = mm(dyb, x2, 1, 1)
        K.dG[q] += dmix[:, :T] * decay[0] + dmix[:, T:] * decay[1]
        return yin, dxd, xdb.astype(F32), dyb.astype(F32)

    def reduce_heads(g, first, second=None):
        parts = list(split2(first))
        if second is not None:
            parts += split2(second)
        return mm(jnp.concatenate(parts, axis=1), K.R[g, : 128 * len(parts), :], 1, 0)

    step_tables(K.pdt, 0, 0)
    bc_forward(K.pbc, 0, 0, lambda lanes: jnp.zeros((8, 128), F32))

    def prompt_pre(g):
        lanes = lanes_of(g)
        xc, gp = conv(K.px[:, lanes].astype(F32), jnp.zeros((8, 128), F32), taps(K.cw, lanes))
        K.pxc[:, lanes] = xc
        K.pgp[:, lanes] = gp
        cum = cum_pair(0, g)
        xw = jnp.exp(cum[T - 1 : T, :] - cum) * (K.dtE[0:T, lanes] * xc)
        spot = pl.ds(pl.multiple_of(8 * lax.rem(g, 5), 8), 8)
        for i in range(16):
            K.fs[2 * i + g // 5, spot, :] = xw[8 * i : 8 * i + 8, :]

    pl.loop(0, NG)(prompt_pre)
    for c in range(32):
        K.fs[c, 40:48, :] = K.B[0, 8 * (c // 2) : 8 * (c // 2) + 8, 128 * (c % 2) : 128 * (c % 2) + 128]

    wait_all(t1)
    K.th[me] = K.ts[me]
    choose(K.of, K.th, K.tl)
    t2 = spread(lambda p: K.tl.at[p], K.tr.at[me], 1)
    start_all(t2)
    f1 = spread(lambda p: K.fs.at[p], K.fh.at[me], 2)
    start_all(f1)
    K.tr[me] = K.tl[me]
    K.fh[me] = K.fs[me]

    def prompt_local(g):
        lanes = lanes_of(g)
        xc = K.pxc[:, lanes]
        z = K.pz[:, lanes].astype(F32)
        dy = K.pcot[:, lanes].astype(F32) * (z * sigmoid(z))
        yin, dxd, xdr, dyr = attend(0, g, xc, dy, K.dtE[0:T, lanes])
        K.acc[0] += reduce_heads(g, dyr * yin - xdr * dxd, xc * dxd)
        K.pdxd[:, lanes] = dxd
        K.pdy[:, lanes] = dy
        K.dD[:, lanes] += fold8(dy * xc)

    def resp_tables(j):
        step_tables(K.rdt, j, j + 1)

    pl.loop(0, 4)(resp_tables)
    wait_all(t2)
    K.tailx[...] = jnp.zeros((8, CHD), F32)
    K.tailb[...] = jnp.zeros((8, BCW), F32)
    for r in range(42):
        i, m = divmod(r, 14)
        row = K.tr[r // 2, r % 2 : r % 2 + 1, :]
        if m < 10:
            K.tailx[5 + i : 6 + i, 128 * m : 128 * m + 128] = row
        else:
            K.tailb[5 + i : 6 + i, 128 * (m - 10) : 128 * (m - 10) + 128] = row

    def resp_bc(j):
        bc_forward(K.rbc, j, j + 1, lambda lanes: K.tailb[:, lanes])

    def resp_local(j, g):
        lanes = lanes_of(g)
        rows = rows_of(j)
        w = taps(K.cw, lanes)
        xc, gp = conv(K.rx[rows, lanes].astype(F32), K.tailx[:, lanes], w)
        z = K.rz[rows, lanes].astype(F32)
        live = jnp.where(iota((T, 128), 0) < K.rlen[0, j], z * sigmoid(z), 0.0)
        dy = K.rcot[rows, lanes].astype(F32) * live
        dt = K.dtE[rows_of(j + 1), lanes]
        yin, dxd, xdr, dyr = attend(j + 1, g, xc, dy, dt)
        K.acc[j + 1] += reduce_heads(g, dyr * yin - xdr * dxd, xc * dxd)
        gain = K.dex[:, lanes]
        K.yl[rows, lanes] = yin + gain * xc
        K.dD[:, lanes] += fold8(dy * xc)
        e = jnp.exp(cum_pair(j + 1, g))
        K.ee[rows, lanes] = e
        K.edy[rows, lanes] = (e * dy).astype(BF)
        dx = conv_back((dt * dxd + gain * dy) * gp, w, K.dw, lanes, K.dtailx)
        K.o_rdx[rows, lanes] = dx.astype(BF)

    def resp_range(lo, hi):
        def one(i):
            resp_local(i // NG, lax.rem(i, NG))

        pl.loop(lo, hi)(one)

    pl.loop(0, 4)(resp_bc)
    resp_range(0, NG)
    wait_all(f1)
    choose(K.of, K.fh, K.fl)
    f2 = spread(lambda p: K.fl.at[p], K.fr.at[me], 3)
    start_all(f2)
    K.fr[me] = K.fl[me]
    resp_range(NG, 4 * NG)

    def state_grad(g):
        lanes = lanes_of(g)
        K.dS[lanes, :] = mm(K.edy[:, lanes], K.Cb[1:5].reshape(4 * T, NS), 0, 0).astype(BF)

    pl.loop(0, NG)(state_grad)
    wait_all(f2)

    def gather_rows(ref, k):
        spot = pl.ds(pl.multiple_of(8 * k, 8), 8)
        return [jnp.concatenate([ref[2 * i + half, spot, :] for i in range(16)], axis=0) for half in range(2)]

    b_halves = gather_rows(K.fr, 5)
    bp = jnp.concatenate(b_halves, axis=1)
    bph, bpl = split2(bp)

    def back(k, dbp):
        halves = gather_rows(K.fr, k)
        for half in range(2):
            g = 5 * half + k
            lanes = lanes_of(g)
            xh, xl = split2(halves[half])
            K.S[lanes, :] = (mm(xh, bph, 0, 0) + mm(xh, bpl, 0, 0) + mm(xl, bph, 0, 0)).astype(BF)
            dSg = K.dS[lanes, :]
            u = mm(bph, dSg, 1, 1)
            dbp = dbp + mm(xh, dSg, 1, 0)
            spot = pl.ds(pl.multiple_of(8 * k, 8), 8)
            for i in range(16):
                K.bs[2 * i + half, spot, :] = u[8 * i : 8 * i + 8, :]
        return dbp

    dbp = lax.fori_loop(0, 5, back, jnp.zeros((T, NS), F32))
    for c in range(32):
        K.bs[c, 40:48, :] = dbp[8 * (c // 2) : 8 * (c // 2) + 8, 128 * (c % 2) : 128 * (c % 2) + 128]
    b1 = spread(lambda p: K.bs.at[p], K.bh.at[me], 4)
    start_all(b1)
    K.bh[me] = K.bs[me]

    def resp_state(i):
        j = i // NG
        g = lax.rem(i, NG)
        lanes = lanes_of(g)
        rows = rows_of(j)
        cs = mm(K.Cb[j + 1], K.S[lanes, :], 1, 1)
        z = K.rz[rows, lanes].astype(F32)
        y = K.yl[rows, lanes] + K.ee[rows, lanes] * cs
        K.o_out[rows, lanes] = (y * (z * sigmoid(z))).astype(BF)
        K.acc[j + 1] += reduce_heads(g, K.edy[rows, lanes].astype(F32) * cs)

    pl.loop(0, 4 * NG)(resp_state)

    def bc_back(bc_ref, at, q, tail, dc_more, db_more, o_ref, tail_ref):
        dgm = jnp.where(lower, K.dG[q], 0.0)
        dc = mm3(dgm, K.B[q], 1, 0) + dc_more
        db = mm3(dgm, K.C[q], 0, 0) + db_more
        for m in range(4):
            lanes = slice(128 * m, 128 * m + 128)
            d = db[:, lanes] if m < 2 else dc[:, 128 * (m - 2) : 128 * (m - 2) + 128]
            K.xs[0:8, :] = tail(lanes)
            K.xs[8:136, :] = bc_ref[rows_of(at), lanes].astype(F32)
            o_ref[rows_of(at), lanes] = conv_back(
                d * K.gpb[rows_of(q), lanes], taps(K.cbc, lanes), K.dwb, lanes, tail_ref
            )

    def resp_bc_back(j):
        more = mm(K.edy[rows_of(j), :], K.S[...], 1, 0)
        bc_back(K.rbc, j, j + 1, lambda lanes: K.tailb[:, lanes], more, 0.0, K.rsum, K.dtailb)

    pl.loop(0, 4)(resp_bc_back)

    K.us[...] = jnp.zeros((32, 2, 128), F32)
    for r in range(42):
        i, m = divmod(r, 14)
        if m < 10:
            row = K.dtailx[5 + i : 6 + i, 128 * m : 128 * m + 128]
        else:
            row = K.dtailb[5 + i : 6 + i, 128 * (m - 10) : 128 * (m - 10) + 128]
        K.us[r // 2, r % 2 : r % 2 + 1, :] = row
    u1 = spread(lambda p: K.us.at[p], K.uh.at[me], 5)
    start_all(u1)
    K.uh[me] = K.us[me]

    core = lax.rem(mt, 2)
    mate = mt + 1 - 2 * core
    across = lax.rem(mt + 2, 4)

    def tensor_copy(src, dst, at, peer):
        return pltpu.make_async_remote_copy(
            src_ref=src, dst_ref=dst, send_sem=K.tsem.at[at, 0], recv_sem=K.tsem.at[at, 1],
            device_id={"tensor": peer}, device_id_type=pl.DeviceIdType.MESH,
        )

    def tensor_sum(buf, recv, full, half, at):
        mine = pl.ds(pl.multiple_of(core * half, 8), half)
        other = pl.ds(pl.multiple_of((1 - core) * half, 8), half)
        steps = [
            tensor_copy(buf.at[other, :], recv.at[0], at, mate),
            tensor_copy(buf.at[mine, :], recv.at[1], at + 1, across),
            tensor_copy(buf.at[mine, :], full.at[mine, :], at + 2, mate),
        ]

        def add(slot):
            def one(i):
                spot = pl.ds(pl.multiple_of(core * half + i * 8, 8), 8)
                buf[spot, :] += recv[slot, pl.ds(pl.multiple_of(i * 8, 8), 8), :]

            pl.loop(0, half // 8)(one)

        def keep():
            if n == 1:
                full[...] = buf[...]
            else:
                full[mine, :] = buf[mine, :]

        return steps, add, keep

    rsteps, radd, rkeep = tensor_sum(K.rsum, K.rrecv, K.o_rdbc, 256, 0)
    if n > 1:
        rsteps[0].start()

    wait_all(b1)
    choose(K.inv, K.bh, K.bl)
    b2 = spread(lambda p: K.bl.at[p], K.br.at[me], 6)
    start_all(b2)
    K.br[me] = K.bl[me]
    wait_all(u1)
    choose(K.inv, K.uh, K.ul)
    u2 = spread(lambda p: K.ul.at[p], K.ur.at[me], 7)
    start_all(u2)
    K.ur[me] = K.ul[me]

    if n > 1:
        rsteps[0].wait()
        radd(0)
        rsteps[1].start()

    pl.loop(0, NG)(prompt_local)

    def steps_back(q, at, o_ref, extra):
        a = K.acc[q].T
        dlr = mmx(a[0:NH, :], trir, 1, 0)
        if extra:
            dlr = dlr + mmx(K.accq[...].T[0:NH, :], tris, 1, 0)
        draw = (a[32 : 32 + NH, :] + K.col[0] * dlr) * K.sig[q]
        o_ref[:, pl.ds(pl.multiple_of(at * T, T), T)] = draw
        K.dlr[...] += K.lr[q] * dlr
        K.ddr[...] += draw

    pl.loop(0, 4)(lambda j: steps_back(j + 1, j, K.o_rddt, False))
    wait_all(b2)
    wait_all(u2)
    if n > 1:
        rsteps[1].wait()
        radd(1)
        rsteps[2].start()
    rkeep()

    for r in range(42):
        i, m = divmod(r, 14)
        row = K.ur[r // 2, r % 2 : r % 2 + 1, :]
        if m < 10:
            K.dtailx[5 + i : 6 + i, 128 * m : 128 * m + 128] = row
        else:
            K.dtailb[5 + i : 6 + i, 128 * (m - 10) : 128 * (m - 10) + 128] = row

    def prompt_final(k):
        halves = gather_rows(K.br, k)
        for half in range(2):
            g = 5 * half + k
            lanes = lanes_of(g)
            w = taps(K.cw, lanes)
            cum = cum_pair(0, g)
            lu = jnp.exp(cum[T - 1 : T, :] - cum) * halves[half]
            dt = K.dtE[0:T, lanes]
            xc = K.pxc[:, lanes]
            xlu = xc * lu
            K.accq[...] += reduce_heads(g, dt * xlu)
            K.acc[0] += reduce_heads(g, jnp.zeros_like(xlu), xlu)
            dxd = K.pdxd[:, lanes] + lu
            dv = (dt * dxd + K.dex[:, lanes] * K.pdy[:, lanes]) * K.pgp[:, lanes]
            K.xs[0:8, :] = jnp.zeros((8, 128), F32)
            K.xs[8:136, :] = K.px[:, lanes].astype(F32)
            dx = conv_back(dv, w, K.dw, lanes, None)
            K.ds[8:136, :] = dx
            K.ds[128:136, :] += K.dtailx[:, lanes]
            K.o_pdx[:, lanes] = K.ds[8:136, :].astype(BF)

    pl.loop(0, 5)(prompt_final)
    db_more = jnp.concatenate(gather_rows(K.br, 5), axis=1)
    bc_back(K.pbc, 0, 0, lambda lanes: jnp.zeros((8, 128), F32), 0.0, db_more, K.psum, None)
    K.psum[120:128, :] += K.dtailb[...]
    K.psum[128:144, :] = jnp.zeros((16, BCW), F32)
    for k in range(4):
        K.psum[128 + k : 129 + k, :] = jnp.sum(K.dwb[k], axis=0, keepdims=True)
    psteps, padd, pkeep = tensor_sum(K.psum, K.precv, K.pfull, 72, 3)
    if n > 1:
        psteps[0].start()
    steps_back(0, 0, K.o_pddt, True)
    if n > 1:
        psteps[0].wait()
        padd(0)
        psteps[1].start()

    K.ps[...] = jnp.zeros((32, 2, 128), F32)

    def put(r, row):
        K.ps[r // 2, r % 2 : r % 2 + 1, :] = row

    for k in range(4):
        total = jnp.sum(K.dw[k], axis=0, keepdims=True)
        for g in range(NG):
            put(k * NG + g, total[:, 128 * g : 128 * g + 128])
    skip = jnp.zeros((8, 128), F32)
    for g in range(NG):
        skip = skip + mm(jnp.concatenate(split2(K.dD[:, 128 * g : 128 * g + 128]), axis=1), K.R[g, :256, :], 1, 0)
    spread_eye = iota((NH, 128), 0) == iota((NH, 128), 1)

    def as_row(ref):
        total = jnp.sum(ref[...], axis=1, keepdims=True)
        return jnp.sum(jnp.where(spread_eye, jnp.broadcast_to(total, (NH, 128)), 0.0), axis=0, keepdims=True)

    put(56, as_row(K.dlr))
    put(57, as_row(K.ddr))
    put(58, jnp.sum(skip, axis=0, keepdims=True))
    if n > 1:
        rsteps[2].wait()
        psteps[1].wait()
        padd(1)
        psteps[2].start()
        psteps[2].wait()
    pkeep()
    for k in range(4):
        for m in range(4):
            put(40 + 4 * k + m, K.pfull[128 + k : 129 + k, 128 * m : 128 * m + 128])
    K.o_pdbc[...] = K.pfull[0:128, :]
    if n > 1:
        p1 = spread(lambda p: K.ps.at[p], K.ph.at[me], 0)
        start_all(p1)
        K.ph[me] = K.ps[me]
        wait_all(p1)
        K.pr[me] = jnp.sum(K.ph[...], axis=0)
        p2 = spread(lambda p: K.pr.at[me], K.pr.at[me], 1)
        start_all(p2)
        wait_all(p2)
    else:
        K.pr[...] = K.ps[...]
    for k in range(4):
        for g in range(NG):
            r = k * NG + g
            K.o_cw[k : k + 1, 128 * g : 128 * g + 128] = K.pr[r // 2, r % 2 : r % 2 + 1, :]
        for m in range(4):
            r = 40 + 4 * k + m
            K.o_cbc[k : k + 1, 128 * m : 128 * m + 128] = K.pr[r // 2, r % 2 : r % 2 + 1, :]
    for i in range(3):
        r = 56 + i
        K.o_hp[i : i + 1, :] = K.pr[r // 2, r % 2 : r % 2 + 1, 0:NH]


def body(n, nt, *args):
    (px, pbc, pdt, pz, rx, rbc, rdt, rz, cw, cbc, hp, of, rlen, pcot, rcot) = args
    inv = jnp.sum(
        jnp.where(of[:, None] == jnp.arange(n)[None, :], jnp.arange(n, dtype=jnp.int32)[:, None], 0), axis=0
    ).astype(jnp.int32)
    table = scratch_table(32)
    vm = pl.BlockSpec(memory_space=pltpu.VMEM)
    sm = pl.BlockSpec(memory_space=pltpu.SMEM)
    shape = jax.ShapeDtypeStruct
    if n == 1:
        of = jnp.arange(32, dtype=jnp.int32)
        inv = of
    params = dict(vmem_limit_bytes=60 * 1024 * 1024, has_side_effects=True)
    if n > 1:
        params["collective_id"] = 0
    return pl.pallas_call(
        functools.partial(kernel, n, nt),
        out_shape=(
            shape((512, CHD), BF), shape((T, CHD), BF), shape((T, BCW), F32), shape((NH, T), F32),
            shape((512, CHD), BF), shape((512, BCW), F32), shape((NH, 512), F32),
            shape((4, CHD), F32), shape((4, BCW), F32), shape((3, NH), F32),
        ),
        in_specs=[vm] * 13 + [sm] * 3,
        out_specs=[vm] * 10,
        scratch_shapes=list(table.values()),
        compiler_params=pltpu.CompilerParams(**params),
    )(px, pbc, pdt, pz, pcot, rx, rbc, rdt, rz, rcot, cw, cbc, hp, of, inv, rlen)


def solution(mesh):
    n = mesh.shape["dp"]
    nt = mesh.shape["tensor"]
    placed = (
        P("dp", "tensor"), P("dp", None), P("tensor", "dp"), P("dp", "tensor"),
        P("dp", "tensor"), P("dp", None), P("tensor", "dp"), P("dp", "tensor"),
        P(None, "tensor"), P(), P(None, "tensor"), P(), P("dp", None),
        P("dp", "tensor"), P("dp", "tensor"),
    )
    return jax.shard_map(
        functools.partial(body, n, nt),
        mesh=mesh,
        in_specs=placed,
        out_specs=(
            P("dp", "tensor"), P("dp", "tensor"), P("dp", None), P("tensor", "dp"),
            P("dp", "tensor"), P("dp", None), P("tensor", "dp"),
            P(None, "tensor"), P(), P(None, "tensor"),
        ),
        check_vma=False,
    )
```

time: 749 us -> 127 us (0.17); the launches traced: 738 us -> 126 us
  blocking collectives: 183 us -> 0 us
  other arithmetic: 154 us -> 1.25 us
  local copies, waits for them, and re-layouts: 142 us -> 9.72 us
  Pallas kernels: 0 us -> 115 us
  matrix products: 109 us -> 0 us
  waiting for transfers between devices: 99 us -> 0 us
  starting transfers between devices: 31.5 us -> 0 us
  between operations: 15.7 us -> 0.7 us
    psum x1 -> x0, blocking collectives: 183 us -> none  [body(): lax.psum((d_conv_feat_r + d_conv_feat_p, conv_proj_part, d_rparams + d_pp...]
    pallas_call x0 -> x1, Pallas kernels: none -> 115 us  [body(): pl.pallas_call(functools.partial(kernel, n, nt), out_shape=(shape((512, C...]
    dot_general x62 -> x0, matrix products: 109 us -> none  [the longest x14 48.4 us: advance(): jnp.einsum('hts,shp->thp', mixing, feat_rows, precision=lax.Precision.HIG...]
    all_to_all x4 -> x0, waiting for transfers between devices: 67 us -> none  [the longest x2 42.2 us: relay_states(): lax.all_to_all(joined.reshape(members, -1), 'dp', split_axis=0, concat_ax...]
    dynamic_update_slice x48 -> x0, other arithmetic: 51.3 us -> none  [the longest x36 42.9 us: conv_all(): lax.map(lambda single: conv_silu(single, trailing_rows, kernel), raw_set)]
    psum x2 -> x0, waiting for transfers between devices: 31.9 us -> none  [the longest x1 23.5 us: body(): d_ppconv = lax.psum(d_ppconv, 'tensor')]
    all_to_all x4 -> x0, starting transfers between devices: 31.3 us -> none  [the longest x2 20.5 us: relay_states(): lax.all_to_all(joined.reshape(members, -1), 'dp', split_axis=0, concat_ax...]
    another operation x25 -> x0, local copies, waits for them, and re-layouts: 27.9 us -> none
  transfers between devices with their start and end apart: 6 -> 0, of which waited for: 6 -> 0; matrix products, arithmetic and copies ran while one was open for 6% -> 0% of each run, Pallas kernels for 0% -> 0%
where the time goes in v1:
time: 127 us; the launch traced here: 126 us
  Pallas kernels  115 us (91%)
  local copies, waits for them, and re-layouts  9.72 us (8%)
    pallas_call x1, Pallas kernels, body(): pl.pallas_call(functools.partial(kernel, n, nt), out_shape=(shape((512, C...  115 us
    unnamed x28, local copies, waits for them, and re-layouts  9.72 us

profile of v1, /device:TPU:0, one launch (start us, length us, event | category | flops | bytes accessed | tf_op | source)
XLA Modules:
  0.0 126.4 jit_solution(10174650078536018694)
XLA Ops:
  0.6 1.3 select_reduce_fusion.refs_14_
  1.9 114.7 %shard_map.222 = (bf16[512,1280]{1,0:T(8,128)(2,1)}, bf16[128,1280]{1,0:T(8,128)(2,1)}, f32[128,512]{1,0:T(8,128)}, f32[20,128]{1,0:T(8,128)}, bf16[512,1280]{1,...) custom-call(bf16[128,1280]{1,0:T(8,128)(2,1)} %refs_0_.1, ...), custom_call_target="tpu_custom_call" | custom-call | tf_op jit(solution)/shard_map/pallas_call | solution.py:652
  116.6 0.0 copy-start.2
  116.6 0.0 copy-start.3
  116.7 0.0 copy-start.6
  116.7 0.0 copy-start
  116.7 2.6 %copy.35 = bf16[512,1280]{1,0:T(8,128)(2,1)} copy(bf16[512,1280]{1,0:T(8,128)(2,1)} %get-tuple-element.20) | data formatting | bytes 2621440
  119.3 0.0 copy-done.2
  119.3 0.7 copy.36
  120.0 0.0 copy-done.3
  120.0 0.7 copy.37
  120.7 0.0 copy-done.6
  120.7 0.6 copy.38
  121.3 0.0 copy-done
  121.3 1.1 copy.39
  122.4 0.6 copy-done.1
  123.0 1.0 copy.40
  124.0 0.0 copy-done.4
  124.0 0.6 copy.41
  124.6 0.0 copy-done.5
  124.6 0.6 copy.42
  125.2 0.0 copy-done.7
  125.2 0.6 copy.43
  125.8 0.6 copy.44
  (6 shorter events, 0.0 us)
Async XLA Ops:
  116.6 2.6 %copy-start.2 = (bf16[128,1280]{1,0:T(8,128)(2,1)S(1)}, bf16[128,1280]{1,0:T(8,128)(2,1)}, u32[]{:S(2)}) copy-start(bf16[128,1280]{1,0:T(8,128)(2,1)} %get-tuple-element.21) | copy-start | bytes 983044
  116.6 3.3 %copy-start.3 = (f32[128,512]{1,0:T(8,128)S(1)}, f32[128,512]{1,0:T(8,128)}, u32[]{:S(2)}) copy-start(f32[128,512]{1,0:T(8,128)} %get-tuple-element.22) | copy-start | bytes 786436
  116.7 4.0 %copy-start.6 = (f32[20,128]{1,0:T(8,128)S(1)}, f32[20,128]{1,0:T(8,128)}, u32[]{:S(2)}) copy-start(f32[20,128]{1,0:T(8,128)} %get-tuple-element.23) | copy-start | bytes 30724
  116.7 4.6 %copy-start = (bf16[512,1280]{1,0:T(8,128)(2,1)S(1)}, bf16[512,1280]{1,0:T(8,128)(2,1)}, u32[]{:S(2)}) copy-start(bf16[512,1280]{1,0:T(8,128)(2,1)} %get-tuple-element.24) | copy-start | bytes 3932164
  121.3 1.7 %copy-start.1 = (f32[512,512]{1,0:T(8,128)S(1)}, f32[512,512]{1,0:T(8,128)}, u32[]{:S(2)}) copy-start(f32[512,512]{1,0:T(8,128)} %get-tuple-element.25) | copy-start | bytes 3145732
  123.0 1.0 copy-start.4
  123.0 1.6 %copy-start.5 = (f32[4,1280]{1,0:T(4,128)S(1)}, f32[4,1280]{1,0:T(4,128)}, u32[]{:S(2)}) copy-start(f32[4,1280]{1,0:T(4,128)} %get-tuple-element.27) | copy-start | bytes 61444
  123.0 2.2 %copy-start.7 = (f32[4,512]{1,0:T(4,128)S(1)}, f32[4,512]{1,0:T(4,128)}, u32[]{:S(2)}) copy-start(f32[4,512]{1,0:T(4,128)} %get-tuple-element.28) | copy-start | bytes 24580
  123.0 2.8 %copy-start.8 = (f32[3,20]{1,0:T(4,128)S(1)}, f32[3,20]{1,0:T(4,128)}, u32[]{:S(2)}) copy-start(f32[3,20]{1,0:T(4,128)} %get-tuple-element.29) | copy-start | bytes 724
